TPU v7x, 256 devices: a whole 4x4x8 slice. The times are simulated.
256 devices in a mesh: dp: 16 (over z_hi, x, core), slot: 4 (over y), hid: 4 (over z_lo).
Axes of the slice: x: 4, y: 4, z: 8 (z_hi: 2, z_lo: 4; z = z_hi * 4 + z_lo), core: 2. Of those that a mesh axis runs over, the one named last changes fastest.
Arguments:
- master_weights: float32 [8, 3, 768, 2048], P('slot', None, 'hid', 'dp'), may hold values from -0.125 to 0.125
- first_moment: float32 [8, 3, 768, 2048], P('slot', None, 'hid', 'dp'), may hold values from -6 to 6
- second_moment: float32 [8, 3, 768, 2048], P('slot', None, 'hid', 'dp'), may hold values from 1 to 100
- tokens_one: bfloat16 [16384, 2048], P('dp'), may hold values from -6 to 6
- grad_out: bfloat16 [16384, 2048], P('dp'), may hold values from -6 to 6
- route_one: int32 [16384, 2], P('dp'), may hold values from 0 to 7, all different within a row
- prob_one: float32 [16384, 2], P('dp'), may hold values from 0.05 to 0.6
- tokens_two: bfloat16 [16384, 2048], P('dp'), may hold values from -6 to 6
- route_two: int32 [16384, 2], P('dp'), may hold values from 0 to 7, all different within a row
- prob_two: float32 [16384, 2], P('dp'), may hold values from 0.05 to 0.6
- old_order: int32 [8], replicated, may hold values from 0 to 7, each once
- new_order: int32 [8], replicated, may hold values from 0 to 7, each once
Outputs:
- moved_master: float32 [8, 3, 768, 2048], P('slot', None, 'hid', 'dp')
- moved_first: float32 [8, 3, 768, 2048], P('slot', None, 'hid', 'dp')
- moved_second: float32 [8, 3, 768, 2048], P('slot', None, 'hid', 'dp')
- next_output: bfloat16 [16384, 2048], P('dp', ('slot', 'hid'))
Inputs may be any that keep to these rules, and one draw needn't show every extreme that they name: `old_order`: lists each of the 8 experts once. `new_order`: lists each of the 8 experts once. `route_one`: each row names 2 different experts. `route_two`: each row names 2 different experts.
All inputs are finite; a program needn't handle non-finite values.
Results may differ from a plain program's by a relative error of at most 0.017.
Values may be sent and summed in bfloat16 or wider, within the bound.
No kernel may reach another device: no remote copies, remote signals or barrier semaphores. Data moves between devices by JAX's collectives and lax.ppermute only.
A program may use at most 128 MiB of HBM per device.

v0:
```python
import jax
import jax.numpy as jnp
from jax import lax
from jax.sharding import Mesh
from jax.sharding import PartitionSpec as P

DP = ("dp_0", "dp_1", "dp_2")
learn_rate = 0.001
beta_one = 0.9
beta_two = 0.95
epsilon = 1e-08
decay_rate = 0.1


def in_blocks(x, dim, size):
    before, after = (x.shape[:dim], x.shape[dim + 1 :])
    return jnp.moveaxis(x.reshape(*before, size, -1, *after), dim, 0)


def summed_rows(x, chips, core, dim):
    sizes = (lax.axis_size(chips), lax.axis_size(core))
    pieces = in_blocks(x, dim, sizes[0] * sizes[1])
    inside = pieces.shape[1:]
    pieces = pieces.reshape(*sizes, *inside).swapaxes(0, 1).reshape(-1, *inside)
    pieces = lax.psum_scatter(pieces, core, scatter_dimension=0, tiled=True)
    return lax.psum_scatter(pieces, chips, scatter_dimension=0, tiled=True)[0]


def scatter_axes(x, axes, dim):
    if not axes:
        return x
    nearer = lax.psum_scatter(x, axes[0], scatter_dimension=dim, tiled=True)
    return scatter_axes(nearer, axes[1:], dim)


def rows_by(left, right):
    return lax.dot_general(
        left, right, (((1,), (1,)), ((), ())), preferred_element_type=jnp.float32
    )


def cols_by(left, right):
    return lax.dot_general(
        left, right, (((0,), (0,)), ((), ())), preferred_element_type=jnp.float32
    )


def expert_parts(tokens, grad_out, scaling, weights):
    gate_proj = rows_by(tokens, weights[0])
    up_proj = rows_by(tokens, weights[1])
    logistic = jax.nn.sigmoid(gate_proj)
    swish_gate = gate_proj * logistic
    activated = (swish_gate * up_proj).astype(jnp.bfloat16)
    scaled_grad = (scaling[:, None] * grad_out.astype(jnp.float32)).astype(jnp.bfloat16)
    d_activated = rows_by(scaled_grad, weights[2])
    d_gate = (d_activated * up_proj * logistic * (1.0 + gate_proj * (1.0 - logistic))).astype(
        jnp.bfloat16
    )
    d_up = (d_activated * swish_gate).astype(jnp.bfloat16)
    return (d_gate, d_up, activated, scaled_grad)


def expert_out(tokens, scaling, weights):
    gate_proj = rows_by(tokens, weights[0])
    up_proj = rows_by(tokens, weights[1])
    mixed = (scaling[:, None] * gate_proj * jax.nn.sigmoid(gate_proj) * up_proj).astype(
        jnp.bfloat16
    )
    return jnp.dot(mixed, weights[2], preferred_element_type=jnp.float32)


def adamw_update(master, moment_a, moment_b, grad_sum):
    new_a = beta_one * moment_a + (1.0 - beta_one) * grad_sum
    new_b = beta_two * moment_b + (1.0 - beta_two) * grad_sum * grad_sum
    fixed_a = new_a / (1.0 - beta_one**10)
    fixed_b = new_b / (1.0 - beta_two**10)
    new_master = master - learn_rate * (
        fixed_a / (jnp.sqrt(fixed_b) + epsilon) + decay_rate * master
    )
    return (new_master, new_a, new_b)


def coefficients(routes, probs, expert_ids):
    matches = routes[:, :, None] == expert_ids[None, None, :]
    return jnp.sum(jnp.where(matches, probs[:, :, None], 0.0), axis=1)


def per_device(
    master_weights,
    first_moment,
    second_moment,
    tokens_one,
    grad_out,
    route_one,
    prob_one,
    tokens_two,
    route_two,
    prob_two,
    old_order,
    new_order,
):
    local_count = master_weights.shape[0]
    slot_index = lax.axis_index("slot")
    slot_count = lax.axis_size("slot")
    offset = slot_index * local_count
    held_ids = lax.dynamic_slice_in_dim(old_order, offset, local_count)
    shard_weights = master_weights.astype(jnp.bfloat16)
    full_weights = lax.all_gather(shard_weights, DP, axis=3, tiled=True)
    scaling_one = coefficients(route_one, prob_one, held_ids)
    parts = [
        expert_parts(tokens_one, grad_out, scaling_one[:, expert], full_weights[expert])
        for expert in range(local_count)
    ]
    gradients = jnp.stack(
        [
            jnp.stack(
                [
                    cols_by(part[0], tokens_one),
                    cols_by(part[1], tokens_one),
                    cols_by(part[2], part[3]),
                ]
            )
            for part in parts
        ]
    )
    owned_grads = summed_rows(gradients.astype(jnp.bfloat16), ("dp_0", "dp_1"), "dp_2", 3).astype(
        jnp.float32
    )
    new_master, new_a, new_b = adamw_update(
        master_weights, first_moment, second_moment, owned_grads
    )
    positions = jnp.arange(old_order.shape[0], dtype=jnp.int32)
    source = jnp.sum(
        jnp.where(old_order[None, :] == new_order[:, None], positions[None, :], 0), axis=1
    )
    owner_slot = source // local_count
    within = source % local_count
    my_owners = lax.dynamic_slice_in_dim(owner_slot, offset, local_count)
    pick_rows = my_owners * local_count + jnp.arange(local_count, dtype=jnp.int32)

    def outgoing(state_block):
        picked = jnp.take(state_block, within, axis=0)
        return picked.reshape((slot_count, local_count) + state_block.shape[1:])

    arrived = (
        lax.all_to_all(outgoing(new_master), "slot", split_axis=0, concat_axis=0, tiled=True),
        lax.all_to_all(outgoing(new_a), "slot", split_axis=0, concat_axis=0, tiled=True),
        lax.all_to_all(outgoing(new_b), "slot", split_axis=0, concat_axis=0, tiled=True),
    )
    moved_states = tuple(
        (
            jnp.take(
                state_block.reshape((slot_count * local_count,) + state_block.shape[2:]),
                pick_rows,
                axis=0,
            )
            for state_block in arrived
        )
    )
    moved_master, moved_first, moved_second = moved_states
    next_shard = new_master.astype(jnp.bfloat16)
    next_full = lax.all_gather(next_shard, DP, axis=3, tiled=True)
    scaling_two = coefficients(route_two, prob_two, held_ids)
    partial_value = expert_out(tokens_two, scaling_two[:, 0], next_full[0])
    expert = 1
    partial_value = partial_value + expert_out(
        tokens_two, scaling_two[:, expert], next_full[expert]
    )
    mixed_out = scatter_axes(partial_value, ("slot", "hid"), 1).astype(jnp.bfloat16)
    return (moved_master, moved_first, moved_second, mixed_out)


def solution(mesh):
    split = Mesh(
        mesh.devices.reshape(2, 4, 2, mesh.shape["slot"], mesh.shape["hid"]),
        ("dp_0", "dp_1", "dp_2", "slot", "hid"),
    )
    in_specs = (
        P("slot", None, "hid", DP),
        P("slot", None, "hid", DP),
        P("slot", None, "hid", DP),
        P(DP, None),
        P(DP, None),
        P(DP, None),
        P(DP, None),
        P(DP, None),
        P(DP, None),
        P(DP, None),
        P(),
        P(),
    )
    out_specs = (
        P("slot", None, "hid", DP),
        P("slot", None, "hid", DP),
        P("slot", None, "hid", DP),
        P(DP, ("slot", "hid")),
    )
    return jax.shard_map(
        per_device, mesh=split, in_specs=in_specs, out_specs=out_specs, check_vma=False
    )
```

profile of v0, /device:TPU:2, one launch (start us, length us, event | category | flops | bytes accessed | tf_op | source)
XLA Modules:
  0.0 531.8 jit_solution(10620187443816465604)
XLA Ops:
  7.2 1.8 convert_element_type.53
  9.1 0.7 dynamic_slice.6
  9.8 0.8 fusion.54
  10.7 85.3 %all-gather.3.cloned.1.call-done = bf16[2,3,192,2048]{3,2,1,0:T(8,128)(2,1)} async-done(((bf16[2,3,192,128]{3,2,1,0:T(8,128)(2,1)}), bf16[2,3,192,2048]{3,2,1,0:T(8,128)(2,1)}) %all-gather.3.cloned.1.call-update) | async-done | bytes 4718608 | tf_op jit(solution)/shard_map/all_gather | solution.py:108
  96.0 4.1 fusion.24
  100.1 3.9 fusion.23
  104.0 1.3 fusion.15
  105.3 1.6 fusion.3
  107.0 0.5 copy-done.6
  107.5 1.1 fusion.14
  108.6 1.2 fusion.13
  109.8 1.5 fusion.26
  111.4 1.5 fusion.25
  112.9 1.3 fusion.10
  114.2 1.6 fusion.6
  115.8 1.1 fusion.9
  116.9 1.4 fusion.8
  118.4 0.2 copy.31
  118.6 0.2 copy.30
  118.8 0.2 copy.29
  118.9 0.2 copy.28
  119.1 0.2 copy.27
  119.3 0.6 maximum_maximum_fusion
  119.9 3.4 copy.26
  123.3 14.0 %reduce-scatter.5.cloned.1.call-done = bf16[8,2,3,192,128]{4,3,2,1,0:T(8,128)(2,1)} async-done(((bf16[16,2,3,192,128]{4,3,2,1,0:T(8,128)(2,1)}), bf16[8,2,3,192,128]{4,3,2,1,0:T(8,128)(2,1)}) %reduce-scatter.5.cloned.1.call-update) | async-done | bytes 2359312 | tf_op jit(solution)/shard_map/reduce_scatter | solution.py:25
  137.4 105.3 %reduce-scatter.7.cloned.1.call-done = bf16[1,2,3,192,128]{4,3,2,1,0:T(8,128)(2,1)} async-done(((bf16[8,2,3,192,128]{4,3,2,1,0:T(8,128)(2,1)}), bf16[1,2,3,192,128]{4,3,2,1,0:T(8,128)(2,1)}) %reduce-scatter.7.cloned.1.call-update) | async-done | bytes 294928 | tf_op jit(solution)/shard_map/reduce_scatter | solution.py:26
  242.7 2.2 fusion.63
  244.9 78.6 %all-gather.5.cloned.1.call-done = bf16[2,3,192,2048]{3,2,1,0:T(8,128)(2,1)} async-done(((bf16[2,3,192,128]{3,2,1,0:T(8,128)(2,1)}), bf16[2,3,192,2048]{3,2,1,0:T(8,128)(2,1)}) %all-gather.5.cloned.1.call-update) | async-done | bytes 4718608 | tf_op jit(solution)/shard_map/all_gather | solution.py:162
  323.5 4.1 fusion.22
  327.7 2.7 fusion.21
  330.3 8.6 %fusion.19 = f32[1024,2048]{1,0:T(8,128)} fusion(bf16[1024,2048]{1,0:T(8,128)(2,1)} %param.23, bf16[2,3,192,2048]{3,2,1,0:T(8,128)(2,1)} %all-gather.5.cloned.1.call-done, f32[192,1024]{1,0:T(8,128)S(1)} %fusion.22, f32[1024]{0:T(1024)S(1)} %bitcast.109), kind=kOutput, calls=%fused_computation.29 | convolution fusion | flops 1611988992 | bytes 14946304 | tf_op jit(solution)/shard_map/dot_general | solution.py:69
  338.9 11.1 %convolution_add_fusion = f32[1024,2048]{1,0:T(8,128)} fusion(f32[1024,2048]{1,0:T(8,128)} %fusion.19, bf16[1024,2048]{1,0:T(8,128)(2,1)} %param.23, bf16[2,3,192,2048]{3,2,1,0:T(8,128)(2,1)} %all-gather.5.cloned.1.call-done, f32[192,1024]{1,0:T(8,128)S(1)} %fusion.21, f32[1024]{0:T(1024)S(1)} %bitcast.108), kind=kOutput, calls=%fused_computation.11 | convolution fusion | flops 1614086144 | bytes 23334912 | tf_op jit(solution)/shard_map/dot_general | solution.py:69
  350.1 0.6 copy-done.7
  350.7 0.2 select_reduce_fusion
  350.9 2.1 gather_fusion.4
  353.0 2.2 gather_fusion.2
  355.2 2.2 gather_fusion
  357.3 6.7 %broadcast_select_fusion = (f32[8,3,192,128]{3,2,1,0:T(8,128)}, f32[8,3,192,128]{3,2,1,0:T(8,128)S(1)}, f32[8,3,192,128]{3,2,1,0:T(8,128)}) fusion(f32[8,3,192,128]{3,2,1,0:T(8,128)} %gather_fusion.4, pred[8]{0:T(512)(128)(4,1)S(1)} %get-tuple-element.14, f32[8,3,192,128]{3,2,1,0:T(8,128)} %gather_fusion.2, f32[8,3,192,128]{3,2,1,0:T(8,128)} %gather_fusion), kind=kLoop, calls=%fused_computation.31 | loop fusion | flops 1769472 | bytes 14155784 | tf_op jit(solution)/shard_map/jit(_take)/select_n | solution.py:142
  364.0 4.5 all-to-all-start.2
  368.6 85.9 %reduce-scatter.9.cloned.1.call-done = f32[1024,512]{1,0:T(8,128)} async-done(((f32[1024,2048]{1,0:T(8,128)}), f32[1024,512]{1,0:T(8,128)}) %reduce-scatter.9.cloned.1.call-update) | async-done | bytes 2097168 | tf_op jit(solution)/shard_map/reduce_scatter | solution.py:32
  454.6 32.7 %all_to_all.15 = f32[4,2,3,192,128]{4,3,2,1,0:T(8,128)} all-to-all(f32[4,2,3,192,128]{4,3,2,1,0:T(8,128)S(1)} %bitcast.98), channel_id=1, replica_groups=mesh['dp_0'=2,'dp_1'=4,'dp_2'=2,'slot'=4,'hid'=4] {'slot'}, dimensions={0} | all-to-all | bytes 4718592 | tf_op jit(solution)/shard_map/all_to_all | solution.py:147
  487.3 3.6 all-to-all-start
  491.1 2.2 gather_fusion.5
  493.3 2.2 gather_fusion.3
  495.6 23.8 %all-to-all-done = f32[4,2,3,192,128]{4,3,2,1,0:T(8,128)S(1)} async-done(((f32[4,2,3,192,128]{4,3,2,1,0:T(8,128)}), f32[4,2,3,192,128]{4,3,2,1,0:T(8,128)S(1)}, u32[]{:S(2)}, u32[]{:S(2)}) %all-to-all-start) | async-done | bytes 2359328 | tf_op jit(solution)/shard_map/all_to_all | solution.py:146
  519.4 1.4 gather_fusion.1
  520.8 2.4 broadcast_select_fusion.3
  523.1 1.8 convert_element_type.66
  (37 shorter events, 0.7 us)
Async XLA Ops:
  7.2 88.8 %all-gather.3.cloned.1.call-start = ((), (), s32[]{:S(2)}) async-start(), calls=%async_computation.7 | async-start | bytes 5013504 | tf_op jit(solution)/shard_map/all_gather | solution.py:108
  9.1 128.2 %reduce-scatter.5.cloned.1.call-start = ((), (), s32[]{:S(2)}) async-start(), calls=%async_computation.8 | async-start | bytes 7077888 | tf_op jit(solution)/shard_map/reduce_scatter | solution.py:25
  96.0 4.1 copy-start.4
  100.1 3.9 copy-start.5
  105.3 2.2 copy-start.6
  123.2 119.5 %copy-start.1 = (f32[2,3,192,128]{3,2,1,0:T(8,128)S(1)}, f32[2,3,192,128]{3,2,1,0:T(8,128)}, u32[]{:S(2)}) copy-start(f32[2,3,192,128]{3,2,1,0:T(8,128)} %param.16) | copy-start | bytes 1769476
  123.2 119.5 %copy-start.2 = (f32[2,3,192,128]{3,2,1,0:T(8,128)S(1)}, f32[2,3,192,128]{3,2,1,0:T(8,128)}, u32[]{:S(2)}) copy-start(f32[2,3,192,128]{3,2,1,0:T(8,128)} %param.17) | copy-start | bytes 1769476
  123.2 119.5 %copy-start.3 = (f32[2,3,192,128]{3,2,1,0:T(8,128)S(1)}, f32[2,3,192,128]{3,2,1,0:T(8,128)}, u32[]{:S(2)}) copy-start(f32[2,3,192,128]{3,2,1,0:T(8,128)} %param.18) | copy-start | bytes 1769476
  123.2 119.4 %reduce-scatter.7.cloned.1.call-start = ((), (), s32[]{:S(2)}) async-start(), calls=%async_computation.9 | async-start | bytes 2654208 | tf_op jit(solution)/shard_map/reduce_scatter | solution.py:26
  137.3 186.2 %all-gather.5.cloned.1.call-start = ((), (), s32[]{:S(2)}) async-start(), calls=%async_computation.10 | async-start | bytes 5013504 | tf_op jit(solution)/shard_map/all_gather | solution.py:162
  244.9 209.7 %reduce-scatter.9.cloned.1.call-start = ((), (), s32[]{:S(2)}) async-start(), calls=%async_computation.11 | async-start | bytes 10485760 | tf_op jit(solution)/shard_map/reduce_scatter | solution.py:32
  323.5 4.1 copy-start
  350.0 0.7 copy-start.7
  350.0 0.7 copy-start.8
  364.0 90.5 %all-to-all-start.2 = ((f32[4,2,3,192,128]{4,3,2,1,0:T(8,128)}), f32[4,2,3,192,128]{4,3,2,1,0:T(8,128)}, u32[]{:S(2)}, u32[]{:S(2)}) async-start(f32[4,2,3,192,128]{4,3,2,1,0:T(8,128)} %bitcast.99), calls=%async_computation.4 | async-start | bytes 4718592 | tf_op jit(solution)/shard_map/all_to_all | solution.py:148
  368.6 154.6 %reduce-scatter.11.cloned.1.call-start = ((), (), s32[]{:S(2)}) async-start(), calls=%async_computation.12 | async-start | bytes 2621440 | tf_op jit(solution)/shard_map/reduce_scatter | solution.py:32
  487.3 32.1 %all-to-all-start = ((f32[4,2,3,192,128]{4,3,2,1,0:T(8,128)}), f32[4,2,3,192,128]{4,3,2,1,0:T(8,128)S(1)}, u32[]{:S(2)}, u32[]{:S(2)}) async-start(f32[4,2,3,192,128]{4,3,2,1,0:T(8,128)} %bitcast.14), calls=%async_computation.2 | async-start | bytes 4718592 | tf_op jit(solution)/shard_map/all_to_all | solution.py:146
Sparse Core Ops, SparseCore 0:
  11.1 84.8 all-gather.2
  123.4 13.8 reduce-scatter.4
  142.0 100.6 reduce-scatter.6
  245.7 77.8 all-gather.4
  350.2 104.3 reduce-scatter.8
  456.9 48.0 reduce-scatter.10
where the time goes:
time: 532 us
  waiting for transfers between devices  393 us (74%)
  matrix products  48.1 us (9%)
  blocking collectives  32.7 us (6%)
  local copies, waits for them, and re-layouts  18.6 us (3%)
  other arithmetic  16.6 us (3%)
  between operations  14.4 us (3%)
  starting transfers between devices  8.42 us (2%)
    reduce_scatter x1, waiting for transfers between devices, summed_rows(): return lax.psum_scatter(pieces, chips, scatter_dimension=0, tiled=True)[0]  105 us
    reduce_scatter x2, waiting for transfers between devices, scatter_axes(): nearer = lax.psum_scatter(x, axes[0], scatter_dimension=dim, tiled=True)  85.9 us
    all_gather x1, waiting for transfers between devices, per_device(): full_weights = lax.all_gather(shard_weights, DP, axis=3, tiled=True)  85.3 us
    all_gather x1, waiting for transfers between devices, per_device(): next_full = lax.all_gather(next_shard, DP, axis=3, tiled=True)  78.6 us
    all_to_all x1, blocking collectives, per_device(): lax.all_to_all(outgoing(new_a), 'slot', split_axis=0, concat_axis=0, tile...  32.7 us
    all_to_all x1, waiting for transfers between devices, per_device(): lax.all_to_all(outgoing(new_master), 'slot', split_axis=0, concat_axis=0,...  23.8 us
    dot_general x8, matrix products, rows_by(): lax.dot_general(left, right, (((1,), (1,)), ((), ())), preferred_element_...  21.1 us
    dot_general x2, matrix products, expert_out(): return jnp.dot(mixed, weights[2], preferred_element_type=jnp.float32)  19.7 us
  transfers between devices with their start and end apart: 8, of which 6 were waited for; matrix products, arithmetic and copies ran while one was open for 4% of the time, Pallas kernels for 0%

commit v1 on v0

--- a/solution.py
+++ b/solution.py
@@ -105,7 +105,9 @@
     offset = slot_index * local_count
     held_ids = lax.dynamic_slice_in_dim(old_order, offset, local_count)
     shard_weights = master_weights.astype(jnp.bfloat16)
-    full_weights = lax.all_gather(shard_weights, DP, axis=3, tiled=True)
+    block_last = jnp.stack([shard_weights for _ in range(lax.axis_size(DP))])
+    q_next = lax.all_to_all(block_last, DP, 0, 0)
+    full_weights = jnp.concatenate(q_next, 3)
     scaling_one = coefficients(route_one, prob_one, held_ids)
     parts = [
         expert_parts(tokens_one, grad_out, scaling_one[:, expert], full_weights[expert])

time: 532 us -> 581 us (1.092)
  waiting for transfers between devices: 393 us -> 428 us
  starting transfers between devices: 8.42 us -> 20.2 us
  local copies, waits for them, and re-layouts: 18.6 us -> 27.1 us
    all_gather x1 -> x0, waiting for transfers between devices: 85.3 us -> none  [per_device(): full_weights = lax.all_gather(shard_weights, DP, axis=3, tiled=True)]
    all_to_all x0 -> x1, waiting for transfers between devices: none -> 66.4 us  [per_device(): q_next = lax.all_to_all(block_last, DP, 0, 0)]
    reduce_scatter x1, waiting for transfers between devices: 14 us -> 68.4 us  [summed_rows(): pieces = lax.psum_scatter(pieces, core, scatter_dimension=0, tiled=True)]
    all_to_all x0 -> x1, starting transfers between devices: none -> 11.6 us  [per_device(): q_next = lax.all_to_all(block_last, DP, 0, 0)]
    slice x0 -> x7, local copies, waits for them, and re-layouts: none -> 6.17 us  [the longest x3 4.12 us: expert_parts(): d_activated = rows_by(scaled_grad, weights[2])]
where the time goes in v1:
time: 581 us
  waiting for transfers between devices  428 us (74%)
  matrix products  43 us (7%)
  blocking collectives  32.7 us (6%)
  local copies, waits for them, and re-layouts  27.1 us (5%)
  starting transfers between devices  20.2 us (3%)
  other arithmetic  15.1 us (3%)
  between operations  14.1 us (2%)
    reduce_scatter x1, waiting for transfers between devices, summed_rows(): return lax.psum_scatter(pieces, chips, scatter_dimension=0, tiled=True)[0]  105 us
    reduce_scatter x2, waiting for transfers between devices, scatter_axes(): nearer = lax.psum_scatter(x, axes[0], scatter_dimension=dim, tiled=True)  85.9 us
    all_gather x1, waiting for transfers between devices, per_device(): next_full = lax.all_gather(next_shard, DP, axis=3, tiled=True)  78.5 us
    reduce_scatter x1, waiting for transfers between devices, summed_rows(): pieces = lax.psum_scatter(pieces, core, scatter_dimension=0, tiled=True)  68.4 us
    all_to_all x1, waiting for transfers between devices, per_device(): q_next = lax.all_to_all(block_last, DP, 0, 0)  66.4 us
    all_to_all x1, blocking collectives, per_device(): lax.all_to_all(outgoing(new_a), 'slot', split_axis=0, concat_axis=0, tile...  32.7 us
    all_to_all x1, waiting for transfers between devices, per_device(): lax.all_to_all(outgoing(new_master), 'slot', split_axis=0, concat_axis=0,...  23.8 us
    dot_general x2, matrix products, expert_out(): return jnp.dot(mixed, weights[2], preferred_element_type=jnp.float32)  19.7 us
  transfers between devices with their start and end apart: 8, of which 6 were waited for; matrix products, arithmetic and copies ran while one was open for 4% of the time, Pallas kernels for 0%

profile of v1, /device:TPU:2, one launch (start us, length us, event | category | flops | bytes accessed | tf_op | source)
XLA Modules:
  0.0 580.6 jit_solution(12360419744379263703)
XLA Ops:
  7.2 1.1 convert_element_type.53
  8.3 3.4 stack.20
  11.7 11.6 %all-to-all-start = ((bf16[16,2,3,192,128]{4,3,2,1,0:T(8,128)(2,1)}), bf16[16,2,3,192,128]{4,3,2,1,0:T(8,128)(2,1)}, u32[]{:S(2)}, u32[]{:S(2)}) async-start(bf16[16,2,3,192,128]{4,3,2,1,0:T(8,128)(2,1)} %stack.20), calls=%async_computation | async-start | bytes 9437184 | tf_op jit(solution)/shard_map/all_to_all | solution.py:109
  23.6 66.4 %all-to-all-done = bf16[16,2,3,192,128]{4,3,2,1,0:T(8,128)(2,1)} async-done(((bf16[16,2,3,192,128]{4,3,2,1,0:T(8,128)(2,1)}), bf16[16,2,3,192,128]{4,3,2,1,0:T(8,128)(2,1)}, u32[]{:S(2)}, u32[]{:S(2)}) %all-to-all-start) | async-done | bytes 4718624 | tf_op jit(solution)/shard_map/all_to_all | solution.py:109
  89.9 2.9 fusion.78
  92.8 0.5 copy.41
  93.4 0.5 copy.42
  93.9 1.5 fusion.24
  95.4 1.5 fusion.21
  97.0 0.5 copy.40
  97.6 1.6 fusion.3
  99.3 1.3 fusion.15
  100.6 1.1 fusion.14
  101.6 1.2 fusion.13
  102.9 0.5 copy.38
  103.4 1.5 fusion.32
  104.9 0.5 copy.39
  105.4 1.5 fusion.29
  107.0 0.7 copy.37
  107.7 1.6 fusion.6
  109.3 1.3 fusion.10
  110.6 1.1 fusion.9
  111.7 1.1 fusion.8
  113.8 0.6 maximum_maximum_fusion
  114.4 3.4 copy.43
  117.9 68.4 %reduce-scatter.5.cloned.1.call-done = bf16[8,2,3,192,128]{4,3,2,1,0:T(8,128)(2,1)} async-done(((bf16[16,2,3,192,128]{4,3,2,1,0:T(8,128)(2,1)}), bf16[8,2,3,192,128]{4,3,2,1,0:T(8,128)(2,1)}) %reduce-scatter.5.cloned.1.call-update) | async-done | bytes 2359312 | tf_op jit(solution)/shard_map/reduce_scatter | solution.py:25
  186.4 105.3 %reduce-scatter.7.cloned.1.call-done = bf16[1,2,3,192,128]{4,3,2,1,0:T(8,128)(2,1)} async-done(((bf16[8,2,3,192,128]{4,3,2,1,0:T(8,128)(2,1)}), bf16[1,2,3,192,128]{4,3,2,1,0:T(8,128)(2,1)}) %reduce-scatter.7.cloned.1.call-update) | async-done | bytes 294928 | tf_op jit(solution)/shard_map/reduce_scatter | solution.py:26
  291.6 2.2 fusion.75
  294.1 78.5 %all-gather.2.cloned.1.call-done = bf16[2,3,192,2048]{3,2,1,0:T(8,128)(2,1)} async-done(((bf16[2,3,192,128]{3,2,1,0:T(8,128)(2,1)}), bf16[2,3,192,2048]{3,2,1,0:T(8,128)(2,1)}) %all-gather.2.cloned.1.call-update) | async-done | bytes 4718608 | tf_op jit(solution)/shard_map/all_gather | solution.py:164
  372.6 4.1 fusion.38
  376.8 2.7 fusion.37
  379.4 8.6 %fusion.19 = f32[1024,2048]{1,0:T(8,128)} fusion(bf16[1024,2048]{1,0:T(8,128)(2,1)} %param.23, bf16[2,3,192,2048]{3,2,1,0:T(8,128)(2,1)} %all-gather.2.cloned.1.call-done, f32[192,1024]{1,0:T(8,128)S(1)} %fusion.38, f32[1024]{0:T(1024)S(1)} %bitcast.128), kind=kOutput, calls=%fused_computation.29 | convolution fusion | flops 1611988992 | bytes 14946304 | tf_op jit(solution)/shard_map/dot_general | solution.py:69
  388.0 11.1 %convolution_add_fusion = f32[1024,2048]{1,0:T(8,128)} fusion(f32[1024,2048]{1,0:T(8,128)} %fusion.19, bf16[1024,2048]{1,0:T(8,128)(2,1)} %param.23, bf16[2,3,192,2048]{3,2,1,0:T(8,128)(2,1)} %all-gather.2.cloned.1.call-done, f32[192,1024]{1,0:T(8,128)S(1)} %fusion.37, f32[1024]{0:T(1024)S(1)} %bitcast.127), kind=kOutput, calls=%fused_computation.11 | convolution fusion | flops 1614086144 | bytes 23334912 | tf_op jit(solution)/shard_map/dot_general | solution.py:69
  399.2 0.6 copy-done.11
  400.0 2.1 gather_fusion.4
  402.1 2.2 gather_fusion.2
  404.3 2.2 gather_fusion
  406.5 6.7 %broadcast_select_fusion = (f32[8,3,192,128]{3,2,1,0:T(8,128)}, f32[8,3,192,128]{3,2,1,0:T(8,128)S(1)}, f32[8,3,192,128]{3,2,1,0:T(8,128)}) fusion(f32[8,3,192,128]{3,2,1,0:T(8,128)} %gather_fusion.4, pred[8]{0:T(512)(128)(4,1)S(1)} %get-tuple-element.14, f32[8,3,192,128]{3,2,1,0:T(8,128)} %gather_fusion.2, f32[8,3,192,128]{3,2,1,0:T(8,128)} %gather_fusion), kind=kLoop, calls=%fused_computation.31 | loop fusion | flops 1769472 | bytes 14155784 | tf_op jit(solution)/shard_map/jit(_take)/select_n | solution.py:144
  413.1 4.6 all-to-all-start.3
  417.8 85.9 %reduce-scatter.9.cloned.1.call-done = f32[1024,512]{1,0:T(8,128)} async-done(((f32[1024,2048]{1,0:T(8,128)}), f32[1024,512]{1,0:T(8,128)}) %reduce-scatter.9.cloned.1.call-update) | async-done | bytes 2097168 | tf_op jit(solution)/shard_map/reduce_scatter | solution.py:32
  503.7 32.7 %all_to_all.20 = f32[4,2,3,192,128]{4,3,2,1,0:T(8,128)} all-to-all(f32[4,2,3,192,128]{4,3,2,1,0:T(8,128)S(1)} %bitcast.111), channel_id=1, replica_groups=mesh['dp_0'=2,'dp_1'=4,'dp_2'=2,'slot'=4,'hid'=4] {'slot'}, dimensions={0} | all-to-all | bytes 4718592 | tf_op jit(solution)/shard_map/all_to_all | solution.py:149
  536.4 3.6 all-to-all-start.1
  540.2 2.2 gather_fusion.5
  542.4 2.2 gather_fusion.3
  544.7 23.8 %all-to-all-done.1 = f32[4,2,3,192,128]{4,3,2,1,0:T(8,128)S(1)} async-done(((f32[4,2,3,192,128]{4,3,2,1,0:T(8,128)}), f32[4,2,3,192,128]{4,3,2,1,0:T(8,128)S(1)}, u32[]{:S(2)}, u32[]{:S(2)}) %all-to-all-start.1) | async-done | bytes 2359328 | tf_op jit(solution)/shard_map/all_to_all | solution.py:148
  568.5 1.4 gather_fusion.1
  569.9 2.4 broadcast_select_fusion.3
  572.3 1.8 convert_element_type.66
  (50 shorter events, 2.1 us)
Async XLA Ops:
  11.6 11.7 %copy-start.10 = (s32[8]{0:T(128)S(1)}, s32[8]{0:T(128)}, u32[]{:S(2)}) copy-start(s32[8]{0:T(128)} %param.26) | copy-start | bytes 100
  11.6 11.8 %copy-start.4 = (f32[1024,2]{0,1:T(2,128)S(1)}, f32[1024,2]{0,1:T(2,128)}, u32[]{:S(2)}) copy-start(f32[1024,2]{0,1:T(2,128)} %param.25) | copy-start | bytes 24580
  11.7 11.8 %copy-start.5 = (s32[1024,2]{0,1:T(2,128)S(1)}, s32[1024,2]{0,1:T(2,128)}, u32[]{:S(2)}) copy-start(s32[1024,2]{0,1:T(2,128)} %param.24) | copy-start | bytes 24580
  11.7 11.8 %copy-start.6 = (f32[1024,2]{0,1:T(2,128)S(1)}, f32[1024,2]{0,1:T(2,128)}, u32[]{:S(2)}) copy-start(f32[1024,2]{0,1:T(2,128)} %param.22) | copy-start | bytes 24580
  11.7 11.8 %copy-start.7 = (s32[1024,2]{0,1:T(2,128)S(1)}, s32[1024,2]{0,1:T(2,128)}, u32[]{:S(2)}) copy-start(s32[1024,2]{0,1:T(2,128)} %param.21) | copy-start | bytes 24580
  11.7 78.2 %all-to-all-start = ((bf16[16,2,3,192,128]{4,3,2,1,0:T(8,128)(2,1)}), bf16[16,2,3,192,128]{4,3,2,1,0:T(8,128)(2,1)}, u32[]{:S(2)}, u32[]{:S(2)}) async-start(bf16[16,2,3,192,128]{4,3,2,1,0:T(8,128)(2,1)} %stack.20), calls=%async_computation | async-start | bytes 9437184 | tf_op jit(solution)/shard_map/all_to_all | solution.py:109
  23.3 163.0 %reduce-scatter.5.cloned.1.call-start = ((), (), s32[]{:S(2)}) async-start(), calls=%async_computation.8 | async-start | bytes 7077888 | tf_op jit(solution)/shard_map/reduce_scatter | solution.py:25
  89.9 4.0 copy-start.9
  95.4 2.2 copy-start.8
  117.8 173.8 %copy-start.1 = (f32[2,3,192,128]{3,2,1,0:T(8,128)S(1)}, f32[2,3,192,128]{3,2,1,0:T(8,128)}, u32[]{:S(2)}) copy-start(f32[2,3,192,128]{3,2,1,0:T(8,128)} %param.16) | copy-start | bytes 1769476
  117.8 173.9 %copy-start.2 = (f32[2,3,192,128]{3,2,1,0:T(8,128)S(1)}, f32[2,3,192,128]{3,2,1,0:T(8,128)}, u32[]{:S(2)}) copy-start(f32[2,3,192,128]{3,2,1,0:T(8,128)} %param.17) | copy-start | bytes 1769476
  117.8 173.9 %copy-start.3 = (f32[2,3,192,128]{3,2,1,0:T(8,128)S(1)}, f32[2,3,192,128]{3,2,1,0:T(8,128)}, u32[]{:S(2)}) copy-start(f32[2,3,192,128]{3,2,1,0:T(8,128)} %param.18) | copy-start | bytes 1769476
  117.8 173.8 %reduce-scatter.7.cloned.1.call-start = ((), (), s32[]{:S(2)}) async-start(), calls=%async_computation.9 | async-start | bytes 2654208 | tf_op jit(solution)/shard_map/reduce_scatter | solution.py:26
  186.3 186.3 %all-gather.2.cloned.1.call-start = ((), (), s32[]{:S(2)}) async-start(), calls=%async_computation.10 | async-start | bytes 5013504 | tf_op jit(solution)/shard_map/all_gather | solution.py:164
  293.8 209.8 %reduce-scatter.9.cloned.1.call-start = ((), (), s32[]{:S(2)}) async-start(), calls=%async_computation.11 | async-start | bytes 10485760 | tf_op jit(solution)/shard_map/reduce_scatter | solution.py:32
  372.6 4.1 copy-start
  399.1 0.7 copy-start.11
  413.1 90.5 %all-to-all-start.3 = ((f32[4,2,3,192,128]{4,3,2,1,0:T(8,128)}), f32[4,2,3,192,128]{4,3,2,1,0:T(8,128)}, u32[]{:S(2)}, u32[]{:S(2)}) async-start(f32[4,2,3,192,128]{4,3,2,1,0:T(8,128)} %bitcast.112), calls=%async_computation.5 | async-start | bytes 4718592 | tf_op jit(solution)/shard_map/all_to_all | solution.py:150
  417.7 154.5 %reduce-scatter.11.cloned.1.call-start = ((), (), s32[]{:S(2)}) async-start(), calls=%async_computation.12 | async-start | bytes 2621440 | tf_op jit(solution)/shard_map/reduce_scatter | solution.py:32
  536.4 32.1 %all-to-all-start.1 = ((f32[4,2,3,192,128]{4,3,2,1,0:T(8,128)}), f32[4,2,3,192,128]{4,3,2,1,0:T(8,128)S(1)}, u32[]{:S(2)}, u32[]{:S(2)}) async-start(f32[4,2,3,192,128]{4,3,2,1,0:T(8,128)} %bitcast.9), calls=%async_computation.3 | async-start | bytes 4718592 | tf_op jit(solution)/shard_map/all_to_all | solution.py:148
Sparse Core Ops, SparseCore 0:
  117.9 68.3 reduce-scatter.4
  191.0 100.6 reduce-scatter.6
  294.8 77.8 all-gather.1
  399.3 104.3 reduce-scatter.8
  506.0 48.0 reduce-scatter.10
